TPU v7x, 32 devices: a whole 2x2x4 slice. The times are simulated.
32 devices in a mesh: seq: 8 (over z, x), mp: 4 (over y, core).
Axes of the slice: x: 2, y: 2, z: 4, core: 2. Of those that a mesh axis runs over, the one named last changes fastest.
Arguments:
- store_rows: bfloat16 [4096, 4096], P('seq', 'mp'), may hold values from -6 to 6
- norm_gain: float32 [4096], replicated, may hold values from 0.1 to 1.9
- w_query: bfloat16 [4096, 2048], P(None, 'mp'), may hold values from -0.01171875 to 0.01171875
- w_key: bfloat16 [4096, 2048], P(None, 'mp'), may hold values from -0.09375 to 0.09375
- w_value: bfloat16 [4096, 2048], P(None, 'mp'), may hold values from -0.09375 to 0.09375
- w_out: bfloat16 [2048, 4096], P(None, 'mp'), may hold values from -0.125 to 0.125
- rel_bias: float32 [32, 32], P(None, 'mp'), may hold values from -3 to 251
- lengths: int32 [8], replicated, may hold values from 64 to 512, as said below
- slot_map: int32 [8], replicated, may hold values from 0 to 7, each once
- block_passage: int32 [8, 8], replicated, may hold values from 0 to 7, as said below
- block_index: int32 [8, 8], replicated, may hold values from 0 to 7, as said below
Outputs:
- encoded: bfloat16 [4096, 4096], P('seq', 'mp')
Inputs may be any that keep to these rules, and one draw needn't show every extreme that they name: For every passage p and place j there is exactly one store shard s and slot k with block_passage[s, k] = p and block_index[s, k] = j; every row names each passage once. `block_index`: see block_passage. `lengths`: one passage has exactly 512 tokens. `slot_map`: a permutation.
All inputs are finite; a program needn't handle non-finite values.
Results may differ from a plain program's by a relative error of at most 0.0054.
Values may be sent and summed in bfloat16 or wider, within the bound.
A program may use at most 128 MiB of HBM per device.

v0:
```python
import math

import jax
import jax.numpy as jnp
from jax import lax
from jax.experimental import pallas as pl
from jax.experimental.pallas import tpu as pltpu
from jax.sharding import PartitionSpec as P

HEAD = 64
PAIR = 2 * HEAD
BUCKETS = 32
TILE = 128
GROUPS = 8
MAX_DISTANCE = 128
MESH = pl.DeviceIdType.MESH


def magnitude_bucket(magnitude):
    half_count = BUCKETS // 2
    exact_count = BUCKETS // 4
    if magnitude < exact_count:
        return magnitude
    scaled = (
        math.log(magnitude / exact_count)
        / math.log(MAX_DISTANCE / exact_count)
        * (half_count - exact_count)
    )
    return min(exact_count + int(scaled), half_count - 1)


STARTS = [
    next(m for m in range(MAX_DISTANCE + 1) if magnitude_bucket(m) >= bucket)
    for bucket in range(BUCKETS // 2)
]


def partner_of(index, step, count):
    result = index
    bit = 1
    while bit < count:
        if step & bit:
            result = result + bit * (1 - 2 * (lax.div(index, bit) % 2))
        bit *= 2
    return result


def each(count, body, init):
    if count <= 8:
        for at in range(count):
            init = body(at, init)
        return init
    return lax.fori_loop(0, count, body, init)


def kernel(
    seq_count,
    mp_count,
    store,
    gain,
    rel_bias,
    lengths,
    slot_map,
    block_passage,
    block_index,
    w_query,
    w_key,
    w_value,
    w_out,
    out,
    send,
    recv,
    normed,
    w_in,
    w_last,
    split,
    ordered,
    strips,
    contexts,
    total,
    targets,
    places,
    slots,
    first_send,
    first_recv,
    second_send,
    second_recv,
    context_send,
    context_recv,
    weight_sem,
):
    me = lax.axis_index("seq")
    mine = lax.axis_index("mp")
    _, block_rows, width = store.shape
    length = seq_count * block_rows
    heads_width = w_in.shape[2]
    heads_here = heads_width // HEAD
    pairs = heads_width // PAIR
    chips = mp_count // 2
    per_group = seq_count // GROUPS
    half_slots = seq_count // 2
    half_rows = length // 2
    my_chip = mine // 2
    my_core = mine % 2
    core_peer = my_chip * 2 + 1 - my_core

    def chip_peer(step):
        return ((my_chip + step) % chips) * 2 + my_core

    partners = [partner_of(me, step, seq_count) for step in range(seq_count)]

    barrier = pltpu.get_barrier_semaphore()
    for step in range(1, seq_count):
        pl.semaphore_signal(
            barrier, inc=1, device_id={"seq": partners[step]}, device_id_type=MESH
        )
    for step in range(1, mp_count):
        pl.semaphore_signal(
            barrier,
            inc=1,
            device_id={"mp": (mine + step) % mp_count},
            device_id_type=MESH,
        )

    loads = [
        pltpu.make_async_copy(w_query, w_in.at[0], weight_sem.at[0]),
        pltpu.make_async_copy(w_key, w_in.at[1], weight_sem.at[1]),
        pltpu.make_async_copy(w_value, w_in.at[2], weight_sem.at[2]),
        pltpu.make_async_copy(w_out, w_last, weight_sem.at[3]),
    ]
    for load in loads:
        load.start()

    def find_target(at, carry):
        targets[at] = slot_map[block_passage[me, at]]
        return carry

    each(seq_count, find_target, 0)

    for step in range(seq_count):
        partner = partners[step]
        source = each(
            seq_count,
            lambda at, found: jnp.where(targets[at] == partner, at, found),
            jnp.int32(0),
        )
        if step == 0:
            recv[mine, 0] = store[source]
        else:
            send[step] = store[source]

    pl.semaphore_wait(barrier, seq_count - 1 + mp_count - 1)

    def first_copy(step):
        return pltpu.make_async_remote_copy(
            src_ref=send.at[step],
            dst_ref=recv.at[mine, step],
            send_sem=first_send.at[step],
            recv_sem=first_recv.at[step],
            device_id={"seq": partners[step]},
            device_id_type=MESH,
        )

    near = list(range(1, half_slots))
    far = list(range(half_slots, seq_count))
    order = []
    while near or far:
        if near:
            order.append(near.pop(0))
        if far:
            order.append(far.pop(0))
    for step in order:
        first_copy(step).start()

    def second_copy(group, lane, origin, target):
        part = recv.at[origin, pl.ds(group * per_group, per_group)]
        return pltpu.make_async_remote_copy(
            src_ref=part,
            dst_ref=part,
            send_sem=second_send.at[group, lane],
            recv_sem=second_recv.at[group, origin],
            device_id={"mp": target},
            device_id_type=MESH,
        )

    def handle(group):
        for step in range(group * per_group, (group + 1) * per_group):
            if step > 0:
                first_copy(step).wait_recv()
        for step in range(1, chips):
            second_copy(group, step, mine, chip_peer(step)).start()
        second_copy(group, 0, mine, core_peer).start()

    def relay(group):
        for step in range(1, chips):
            origin = chip_peer(step)
            second_copy(group, step, origin, origin).wait_recv()
            second_copy(group, chips - 1 + step, origin, core_peer).start()

    def complete(group):
        for step in range(chips):
            origin = ((my_chip + step) % chips) * 2 + 1 - my_core
            second_copy(group, 0, origin, core_peer).wait_recv()

    handle(0)

    offset = lax.broadcasted_iota(jnp.int32, (1, 4 * TILE), 1) - 2 * TILE
    distance = jnp.abs(offset)

    def make_strip(head, carry):
        before = jnp.full((1, 4 * TILE), rel_bias[0, head], jnp.float32)
        after = jnp.full((1, 4 * TILE), rel_bias[BUCKETS // 2, head], jnp.float32)
        for bucket in range(1, BUCKETS // 2):
            reached = distance >= STARTS[bucket]
            before = jnp.where(reached, rel_bias[bucket, head], before)
            after = jnp.where(reached, rel_bias[BUCKETS // 2 + bucket, head], after)
        line = jnp.where(offset > 0, after, before)
        wide = jnp.broadcast_to(line, (TILE, 4 * TILE))
        rolled = pltpu.roll(wide, 3 * TILE, 1, stride=1, stride_axis=0)
        strips[head] = rolled[:, : 3 * TILE]
        return carry

    lax.fori_loop(0, heads_here, make_strip, 0)

    handle(1)
    relay(0)

    my_passage = each(
        seq_count,
        lambda at, found: jnp.where(slot_map[at] == me, at, found),
        jnp.int32(0),
    )
    valid_length = lengths[my_passage]
    for step in range(seq_count):
        shard = partners[step]
        places[step] = each(
            seq_count,
            lambda at, found: jnp.where(
                block_passage[shard, at] == my_passage, block_index[shard, at], found
            ),
            jnp.int32(0),
        )

    def find_slot(place, carry):
        slots[place] = each(
            seq_count,
            lambda at, found: jnp.where(places[at] == place, at, found),
            jnp.int32(0),
        )
        return carry

    lax.fori_loop(0, seq_count, find_slot, 0)

    handle(2)
    relay(1)
    handle(3)
    relay(2)

    def normalise(half):
        def one(at, carry):
            slot = half * half_slots + at
            square = jnp.zeros((block_rows, 1), jnp.float32)
            for part in range(mp_count):
                x = recv[part, slot].astype(jnp.float32)
                square = square + jnp.sum(x * x, axis=-1, keepdims=True)
            scale = lax.rsqrt(square / (mp_count * width) + 1e-06)
            rows = pl.ds(pl.multiple_of(slot * block_rows, block_rows), block_rows)
            for part in range(mp_count):
                columns = slice(part * width, (part + 1) * width)
                x = recv[part, slot].astype(jnp.float32)
                normed[rows, columns] = (x * scale * gain[:, columns]).astype(jnp.bfloat16)
            return carry

        lax.fori_loop(0, half_slots, one, 0)

    step_width = min(256, heads_width)

    def project(half, which):
        def one(at, carry):
            columns = pl.ds(pl.multiple_of(at * step_width, step_width), step_width)
            product = jnp.dot(
                normed[half * half_rows : (half + 1) * half_rows, :],
                w_in[which, :, columns],
                preferred_element_type=jnp.float32,
            )
            split[which, half * half_slots : (half + 1) * half_slots, :, columns] = (
                product.astype(jnp.bfloat16).reshape(half_slots, block_rows, step_width)
            )
            return carry

        lax.fori_loop(0, heads_width // step_width, one, 0)

    handle(4)
    relay(3)
    for group in range(4):
        complete(group)
    normalise(0)
    handle(5)
    relay(4)
    loads[0].wait()
    project(0, 0)
    handle(6)
    relay(5)
    loads[1].wait()
    project(0, 1)
    handle(7)
    relay(6)
    loads[2].wait()
    project(0, 2)
    relay(7)
    for group in range(4, 8):
        complete(group)
    normalise(1)
    project(1, 0)
    project(1, 1)
    project(1, 2)

    def arrange(place, carry):
        slot = slots[place]
        rows = pl.ds(pl.multiple_of(place * block_rows, block_rows), block_rows)
        for which in range(3):
            block = split[which, slot]
            for pair in range(pairs):
                ordered[which, pair, rows, :] = block[:, pair * PAIR : (pair + 1) * PAIR]
        return carry

    lax.fori_loop(0, seq_count, arrange, 0)

    key_at = lax.broadcasted_iota(jnp.int32, (1, length), 1)
    blocked = jnp.where(key_at < valid_length, 0.0, -jnp.inf).astype(jnp.float32)
    lane = lax.broadcasted_iota(jnp.int32, (1, PAIR), 1)
    lane_masks = [
        jnp.where(lane // HEAD == at, 1.0, 0.0).astype(jnp.bfloat16) for at in range(2)
    ]
    tiles = length // TILE

    def context_copy(pair, lane_at, origin, target):
        part = contexts.at[origin, pair]
        return pltpu.make_async_remote_copy(
            src_ref=part,
            dst_ref=part,
            send_sem=context_send.at[pair, lane_at],
            recv_sem=context_recv.at[pair, origin],
            device_id={"mp": target},
            device_id_type=MESH,
        )

    def context_relay(pair):
        for step in range(1, chips):
            origin = chip_peer(step)
            context_copy(pair, step, origin, origin).wait_recv()
            context_copy(pair, chips - 1 + step, origin, core_peer).start()

    def attend(pair, carry):
        for row_tile in range(tiles):
            rows = slice(row_tile * TILE, (row_tile + 1) * TILE)
            both = []
            for at in range(2):
                head = pair * 2 + at
                scores = lax.dot_general(
                    ordered[0, pair, rows, :] * lane_masks[at],
                    ordered[1, pair],
                    (((1,), (1,)), ((), ())),
                    preferred_element_type=jnp.float32,
                )
                pieces = []
                for key_tile in range(tiles):
                    columns = slice(key_tile * TILE, (key_tile + 1) * TILE)
                    gap = key_tile - row_tile
                    if gap < -1:
                        bias = rel_bias[BUCKETS // 2 - 1, head]
                    elif gap > 1:
                        bias = rel_bias[BUCKETS - 1, head]
                    else:
                        bias = strips[head, :, (gap + 1) * TILE : (gap + 2) * TILE]
                    pieces.append(scores[:, columns] + bias + blocked[:, columns])
                scores = jnp.concatenate(pieces, axis=1)
                weights = jnp.exp(scores - jnp.max(scores, axis=-1, keepdims=True))
                share = 1.0 / jnp.sum(weights, axis=-1, keepdims=True)
                mixed = jnp.dot(
                    weights.astype(jnp.bfloat16),
                    ordered[2, pair],
                    preferred_element_type=jnp.float32,
                )
                both.append(mixed * share)
            contexts[mine, pair, rows, :] = jnp.where(lane < HEAD, both[0], both[1]).astype(
                jnp.bfloat16
            )
        for step in range(1, chips):
            context_copy(pair, step, mine, chip_peer(step)).start()
        context_copy(pair, 0, mine, core_peer).start()

        @pl.when(pair >= 2)
        def _():
            context_relay(pair - 2)

        return carry

    lax.fori_loop(0, pairs, attend, 0)

    out_width = min(256, width)

    def accumulate(origin, first, last):
        rows = pl.ds(pl.multiple_of(origin * heads_width, heads_width), heads_width)

        def one(at, carry):
            columns = pl.ds(pl.multiple_of(at * out_width, out_width), out_width)
            product = jnp.dot(
                jnp.concatenate([contexts[origin, pair] for pair in range(pairs)], axis=1),
                w_last[rows, columns],
                preferred_element_type=jnp.float32,
            )
            if not first:
                product = product + total[:, columns]
            if last:
                out[:, columns] = product.astype(jnp.bfloat16)
            else:
                total[:, columns] = product
            return carry

        lax.fori_loop(0, width // out_width, one, 0)

    loads[3].wait()
    for pair in range(max(0, pairs - 2), pairs - 1):
        context_relay(pair)
    accumulate(mine, True, False)

    def add_residual(place, carry):
        rows = pl.ds(pl.multiple_of(place * block_rows, block_rows), block_rows)
        total[rows, :] = total[rows, :] + recv[mine, slots[place]].astype(jnp.float32)
        return carry

    lax.fori_loop(0, seq_count, add_residual, 0)
    context_relay(pairs - 1)
    for pair in range(pairs):
        context_copy(pair, 0, core_peer, core_peer).wait_recv()
    accumulate(core_peer, False, chips == 1)
    for step in range(1, chips):
        accumulate(chip_peer(step), False, False)
    for step in range(1, chips):
        origin = ((my_chip + step) % chips) * 2 + 1 - my_core
        for pair in range(pairs):
            context_copy(pair, 0, origin, core_peer).wait_recv()
        accumulate(origin, False, step == chips - 1)

    for step in range(1, seq_count):
        first_copy(step).wait_send()
    for group in range(GROUPS):
        for lane_at in range(mp_count - 1):
            second_copy(group, lane_at, mine, core_peer).wait_send()
    for pair in range(pairs):
        for lane_at in range(mp_count - 1):
            context_copy(pair, lane_at, mine, core_peer).wait_send()


def on_device(seq_count, mp_count, *arguments):
    (
        store_rows,
        norm_gain,
        w_query,
        w_key,
        w_value,
        w_out,
        rel_bias,
        lengths,
        slot_map,
        block_passage,
        block_index,
    ) = arguments
    length, width = store_rows.shape
    block_rows = length // seq_count
    features, heads_width = w_query.shape
    heads_here = heads_width // HEAD
    pairs = heads_width // PAIR
    dma = pltpu.SemaphoreType.DMA
    vmem = pl.BlockSpec(memory_space=pltpu.VMEM)
    smem = pl.BlockSpec(memory_space=pltpu.SMEM)
    anywhere = pl.BlockSpec(memory_space=pl.ANY)

    def body(*refs):
        kernel(seq_count, mp_count, *refs)

    return pl.pallas_call(
        body,
        out_shape=jax.ShapeDtypeStruct((length, width), jnp.bfloat16),
        in_specs=[vmem, vmem] + [smem] * 5 + [anywhere] * 4,
        out_specs=vmem,
        scratch_shapes=[
            pltpu.VMEM((seq_count, block_rows, width), jnp.bfloat16),
            pltpu.VMEM((mp_count, seq_count, block_rows, width), jnp.bfloat16),
            pltpu.VMEM((length, features), jnp.bfloat16),
            pltpu.VMEM((3, features, heads_width), jnp.bfloat16),
            pltpu.VMEM(w_out.shape, jnp.bfloat16),
            pltpu.VMEM((3, seq_count, block_rows, heads_width), jnp.bfloat16),
            pltpu.VMEM((3, pairs, length, PAIR), jnp.bfloat16),
            pltpu.VMEM((heads_here, TILE, 3 * TILE), jnp.float32),
            pltpu.VMEM((mp_count, pairs, length, PAIR), jnp.bfloat16),
            pltpu.VMEM((length, width), jnp.float32),
            pltpu.SMEM((seq_count,), jnp.int32),
            pltpu.SMEM((seq_count,), jnp.int32),
            pltpu.SMEM((seq_count,), jnp.int32),
            dma((seq_count,)),
            dma((seq_count,)),
            dma((GROUPS, mp_count - 1)),
            dma((GROUPS, mp_count)),
            dma((pairs, mp_count - 1)),
            dma((pairs, mp_count)),
            dma((4,)),
        ],
        compiler_params=pltpu.CompilerParams(
            collective_id=0, has_side_effects=True, vmem_limit_bytes=56 * 1024 * 1024
        ),
        name="encoder",
    )(
        store_rows.reshape(seq_count, block_rows, width),
        norm_gain.reshape(1, features),
        rel_bias,
        lengths,
        slot_map,
        block_passage,
        block_index,
        w_query,
        w_key,
        w_value,
        w_out,
    )


def solution(mesh):
    placed = (
        P("seq", "mp"),
        P(),
        P(None, "mp"),
        P(None, "mp"),
        P(None, "mp"),
        P(None, "mp"),
        P(None, "mp"),
        P(),
        P(),
        P(),
        P(),
    )

    def run(*arguments):
        return on_device(mesh.shape["seq"], mesh.shape["mp"], *arguments)

    return jax.shard_map(
        run, mesh=mesh, in_specs=placed, out_specs=P("seq", "mp"), check_vma=False
    )
```

profile of v0, /device:TPU:11, one launch (start us, length us, event | category | flops | bytes accessed | tf_op | source)
XLA Modules:
  0.0 66.7 jit_solution(8872656199992750262)
XLA Ops:
  0.0 1.4 %copy.12.refs_2_ = f32[32,8]{1,0:T(8,128)} copy(f32[32,8]{0,1:T(8,128)} %param.17) | data formatting | bytes 2048 | tf_op args[6]
  1.4 63.0 %encoder.1 = bf16[512,1024]{1,0:T(8,128)(2,1)} custom-call(bf16[8,64,1024]{2,1,0:T(8,128)(2,1)} %bitcast.2, f32[1,4096]{1,0:T(1,128)} %bitcast.3, f32[32,8]{1,0:T(8,128)} %copy.12.refs_2_, s32[8]{0:T(128)} %refs_3_.1, s32[8]{0:T(128)} %refs_4_.1, s32[8,8]{1,0:T(8,128)} %refs_5_.1, s32[8,8]{1,0:T(8,128)} %refs_6_.1, bf16[4096,512]{1,0:T(8,128)(2,1)} %refs_7_.1, ...), custom_call_target="tpu_custom_call" | custom-call | tf_op jit(solution)/shard_map/encoder/pallas_call | solution.py:483
  64.4 2.3 %copy.14 = bf16[512,1024]{1,0:T(8,128)(2,1)} copy(bf16[512,1024]{1,0:T(8,128)(2,1)} %encoder.1) | data formatting | bytes 2097152
where the time goes:
time: 67.9 us; the launch traced here: 66.7 us
  Pallas kernels  63 us (93%)
  local copies, waits for them, and re-layouts  3.63 us (5%)
    pallas_call x1, Pallas kernels, on_device(): pl.pallas_call(body, out_shape=jax.ShapeDtypeStruct((length, width), jnp....  63 us
    unnamed x2, local copies, waits for them, and re-layouts  3.63 us

commit v1 on v0

--- a/solution.py
+++ b/solution.py
@@ -56,8 +56,8 @@
 def kernel(
     seq_count,
     mp_count,
-    store,
-    gain,
+    store_rows,
+    gain_row,
     rel_bias,
     lengths,
     slot_map,
@@ -68,6 +68,8 @@
     w_value,
     w_out,
     out,
+    store,
+    gain,
     send,
     recv,
     normed,
@@ -109,6 +111,10 @@
 
     partners = [partner_of(me, step, seq_count) for step in range(seq_count)]
 
+    store_load = pltpu.make_async_copy(store_rows, store, weight_sem.at[4])
+    gain_load = pltpu.make_async_copy(gain_row, gain, weight_sem.at[5])
+    store_load.start()
+    gain_load.start()
     barrier = pltpu.get_barrier_semaphore()
     for step in range(1, seq_count):
         pl.semaphore_signal(
@@ -128,27 +134,22 @@
         pltpu.make_async_copy(w_value, w_in.at[2], weight_sem.at[2]),
         pltpu.make_async_copy(w_out, w_last, weight_sem.at[3]),
     ]
-    for load in loads:
-        load.start()
-
     def find_target(at, carry):
         targets[at] = slot_map[block_passage[me, at]]
         return carry
 
     each(seq_count, find_target, 0)
 
-    for step in range(seq_count):
-        partner = partners[step]
-        source = each(
+    def find_source(step):
+        return each(
             seq_count,
-            lambda at, found: jnp.where(targets[at] == partner, at, found),
+            lambda at, found: jnp.where(targets[at] == partners[step], at, found),
             jnp.int32(0),
         )
-        if step == 0:
-            recv[mine, 0] = store[source]
-        else:
-            send[step] = store[source]
-
+
+    own_source = find_source(0)
+    store_load.wait()
+    recv[mine, 0] = store[own_source]
     pl.semaphore_wait(barrier, seq_count - 1 + mp_count - 1)
 
     def first_copy(step):
@@ -160,17 +161,6 @@
             device_id={"seq": partners[step]},
             device_id_type=MESH,
         )
-
-    near = list(range(1, half_slots))
-    far = list(range(half_slots, seq_count))
-    order = []
-    while near or far:
-        if near:
-            order.append(near.pop(0))
-        if far:
-            order.append(far.pop(0))
-    for step in order:
-        first_copy(step).start()
 
     def second_copy(group, lane, origin, target):
         part = recv.at[origin, pl.ds(group * per_group, per_group)]
@@ -202,18 +192,34 @@
             origin = ((my_chip + step) % chips) * 2 + 1 - my_core
             second_copy(group, 0, origin, core_peer).wait_recv()
 
-    handle(0)
+    near = list(range(1, half_slots))
+    far = list(range(half_slots, seq_count))
+    order = []
+    while near or far:
+        if near:
+            order.append(near.pop(0))
+        if far:
+            order.append(far.pop(0))
+    if per_group == 1:
+        handle(0)
+    for step in order:
+        send[step] = store[find_source(step)]
+        first_copy(step).start()
+    if per_group > 1:
+        handle(0)
+    for load in loads:
+        load.start()
 
     offset = lax.broadcasted_iota(jnp.int32, (1, 4 * TILE), 1) - 2 * TILE
     distance = jnp.abs(offset)
 
     def make_strip(head, carry):
-        before = jnp.full((1, 4 * TILE), rel_bias[0, head], jnp.float32)
-        after = jnp.full((1, 4 * TILE), rel_bias[BUCKETS // 2, head], jnp.float32)
+        before = jnp.full((1, 4 * TILE), rel_bias[head, 0], jnp.float32)
+        after = jnp.full((1, 4 * TILE), rel_bias[head, BUCKETS // 2], jnp.float32)
         for bucket in range(1, BUCKETS // 2):
             reached = distance >= STARTS[bucket]
-            before = jnp.where(reached, rel_bias[bucket, head], before)
-            after = jnp.where(reached, rel_bias[BUCKETS // 2 + bucket, head], after)
+            before = jnp.where(reached, rel_bias[head, bucket], before)
+            after = jnp.where(reached, rel_bias[head, BUCKETS // 2 + bucket], after)
         line = jnp.where(offset > 0, after, before)
         wide = jnp.broadcast_to(line, (TILE, 4 * TILE))
         rolled = pltpu.roll(wide, 3 * TILE, 1, stride=1, stride_axis=0)
@@ -256,9 +262,9 @@
     handle(3)
     relay(2)
 
-    def normalise(half):
+    def normalise(first, count):
         def one(at, carry):
-            slot = half * half_slots + at
+            slot = first * per_group + at
             square = jnp.zeros((block_rows, 1), jnp.float32)
             for part in range(mp_count):
                 x = recv[part, slot].astype(jnp.float32)
@@ -271,60 +277,72 @@
                 normed[rows, columns] = (x * scale * gain[:, columns]).astype(jnp.bfloat16)
             return carry
 
-        lax.fori_loop(0, half_slots, one, 0)
+        lax.fori_loop(0, count * per_group, one, 0)
 
     step_width = min(256, heads_width)
 
-    def project(half, which):
-        def one(at, carry):
-            columns = pl.ds(pl.multiple_of(at * step_width, step_width), step_width)
-            product = jnp.dot(
-                normed[half * half_rows : (half + 1) * half_rows, :],
-                w_in[which, :, columns],
-                preferred_element_type=jnp.float32,
-            )
-            split[which, half * half_slots : (half + 1) * half_slots, :, columns] = (
-                product.astype(jnp.bfloat16).reshape(half_slots, block_rows, step_width)
-            )
-            return carry
-
-        lax.fori_loop(0, heads_width // step_width, one, 0)
+    def project(first, count, which, at):
+        columns = slice(at * step_width, (at + 1) * step_width)
+        part = slice(first * per_group, (first + count) * per_group)
+        product = jnp.dot(
+            normed[part.start * block_rows : part.stop * block_rows, :],
+            w_in[which, :, columns],
+            preferred_element_type=jnp.float32,
+        )
+        split[which, part, :, columns] = product.astype(jnp.bfloat16).reshape(
+            count * per_group, block_rows, step_width
+        )
+
+    steps = heads_width // step_width
+
+    def project_all(first, count, which):
+        for at in range(steps):
+            project(first, count, which, at)
 
     handle(4)
     relay(3)
+    handle(5)
     for group in range(4):
         complete(group)
-    normalise(0)
-    handle(5)
+    gain_load.wait()
+    normalise(0, 4)
+    loads[0].wait()
+    project_all(0, 4, 0)
     relay(4)
-    loads[0].wait()
-    project(0, 0)
+    loads[1].wait()
+    project_all(0, 4, 1)
     handle(6)
+    loads[2].wait()
+    project_all(0, 4, 2)
     relay(5)
-    loads[1].wait()
-    project(0, 1)
+    complete(4)
+    complete(5)
+    normalise(4, 2)
+    project_all(4, 2, 0)
     handle(7)
     relay(6)
-    loads[2].wait()
-    project(0, 2)
+    project_all(4, 2, 1)
+    project_all(4, 2, 2)
     relay(7)
-    for group in range(4, 8):
-        complete(group)
-    normalise(1)
-    project(1, 0)
-    project(1, 1)
-    project(1, 2)
-
-    def arrange(place, carry):
-        slot = slots[place]
-        rows = pl.ds(pl.multiple_of(place * block_rows, block_rows), block_rows)
-        for which in range(3):
-            block = split[which, slot]
-            for pair in range(pairs):
-                ordered[which, pair, rows, :] = block[:, pair * PAIR : (pair + 1) * PAIR]
-        return carry
-
-    lax.fori_loop(0, seq_count, arrange, 0)
+    complete(6)
+    complete(7)
+    normalise(6, 2)
+
+    step_pairs = step_width // PAIR
+
+    def arrange(at):
+        def one(place, carry):
+            slot = slots[place]
+            rows = pl.ds(pl.multiple_of(place * block_rows, block_rows), block_rows)
+            for which in range(3):
+                block = split[which, slot, :, at * step_width : (at + 1) * step_width]
+                for pair in range(step_pairs):
+                    ordered[which, at * step_pairs + pair, rows, :] = block[
+                        :, pair * PAIR : (pair + 1) * PAIR
+                    ]
+            return carry
+
+        lax.fori_loop(0, seq_count, one, 0)
 
     key_at = lax.broadcasted_iota(jnp.int32, (1, length), 1)
     blocked = jnp.where(key_at < valid_length, 0.0, -jnp.inf).astype(jnp.float32)
@@ -334,22 +352,23 @@
     ]
     tiles = length // TILE
 
-    def context_copy(pair, lane_at, origin, target):
-        part = contexts.at[origin, pair]
+    def context_copy(pair, piece, lane_at, origin, target):
+        part = contexts.at[origin, pair, pl.ds(piece * half_rows, half_rows)]
         return pltpu.make_async_remote_copy(
             src_ref=part,
             dst_ref=part,
-            send_sem=context_send.at[pair, lane_at],
-            recv_sem=context_recv.at[pair, origin],
+            send_sem=context_send.at[pair, piece, lane_at],
+            recv_sem=context_recv.at[pair, piece, origin],
             device_id={"mp": target},
             device_id_type=MESH,
         )
 
     def context_relay(pair):
-        for step in range(1, chips):
-            origin = chip_peer(step)
-            context_copy(pair, step, origin, origin).wait_recv()
-            context_copy(pair, chips - 1 + step, origin, core_peer).start()
+        for piece in range(2):
+            for step in range(1, chips):
+                origin = chip_peer(step)
+                context_copy(pair, piece, step, origin, origin).wait_recv()
+                context_copy(pair, piece, chips - 1 + step, origin, core_peer).start()
 
     def attend(pair, carry):
         for row_tile in range(tiles):
@@ -368,9 +387,9 @@
                     columns = slice(key_tile * TILE, (key_tile + 1) * TILE)
                     gap = key_tile - row_tile
                     if gap < -1:
-                        bias = rel_bias[BUCKETS // 2 - 1, head]
+                        bias = rel_bias[head, BUCKETS // 2 - 1]
                     elif gap > 1:
-                        bias = rel_bias[BUCKETS - 1, head]
+                        bias = rel_bias[head, BUCKETS - 1]
                     else:
                         bias = strips[head, :, (gap + 1) * TILE : (gap + 2) * TILE]
                     pieces.append(scores[:, columns] + bias + blocked[:, columns])
@@ -386,9 +405,11 @@
             contexts[mine, pair, rows, :] = jnp.where(lane < HEAD, both[0], both[1]).astype(
                 jnp.bfloat16
             )
-        for step in range(1, chips):
-            context_copy(pair, step, mine, chip_peer(step)).start()
-        context_copy(pair, 0, mine, core_peer).start()
+            if (row_tile + 1) % (tiles // 2) == 0:
+                piece = row_tile // (tiles // 2)
+                for step in range(1, chips):
+                    context_copy(pair, piece, step, mine, chip_peer(step)).start()
+                context_copy(pair, piece, 0, mine, core_peer).start()
 
         @pl.when(pair >= 2)
         def _():
@@ -396,7 +417,11 @@
 
         return carry
 
-    lax.fori_loop(0, pairs, attend, 0)
+    for at in range(steps):
+        for which in range(3):
+            project(6, 2, which, at)
+        arrange(at)
+        lax.fori_loop(at * step_pairs, (at + 1) * step_pairs, attend, 0)
 
     out_width = min(256, width)
 
@@ -433,14 +458,16 @@
     lax.fori_loop(0, seq_count, add_residual, 0)
     context_relay(pairs - 1)
     for pair in range(pairs):
-        context_copy(pair, 0, core_peer, core_peer).wait_recv()
+        for piece in range(2):
+            context_copy(pair, piece, 0, core_peer, core_peer).wait_recv()
     accumulate(core_peer, False, chips == 1)
     for step in range(1, chips):
         accumulate(chip_peer(step), False, False)
     for step in range(1, chips):
         origin = ((my_chip + step) % chips) * 2 + 1 - my_core
         for pair in range(pairs):
-            context_copy(pair, 0, origin, core_peer).wait_recv()
+            for piece in range(2):
+                context_copy(pair, piece, 0, origin, core_peer).wait_recv()
         accumulate(origin, False, step == chips - 1)
 
     for step in range(1, seq_count):
@@ -449,8 +476,9 @@
         for lane_at in range(mp_count - 1):
             second_copy(group, lane_at, mine, core_peer).wait_send()
     for pair in range(pairs):
-        for lane_at in range(mp_count - 1):
-            context_copy(pair, lane_at, mine, core_peer).wait_send()
+        for piece in range(2):
+            for lane_at in range(mp_count - 1):
+                context_copy(pair, piece, lane_at, mine, core_peer).wait_send()
 
 
 def on_device(seq_count, mp_count, *arguments):
@@ -483,9 +511,11 @@
     return pl.pallas_call(
         body,
         out_shape=jax.ShapeDtypeStruct((length, width), jnp.bfloat16),
-        in_specs=[vmem, vmem] + [smem] * 5 + [anywhere] * 4,
+        in_specs=[anywhere] * 2 + [smem] * 5 + [anywhere] * 4,
         out_specs=vmem,
         scratch_shapes=[
+            pltpu.VMEM((seq_count, block_rows, width), jnp.bfloat16),
+            pltpu.VMEM((1, features), jnp.float32),
             pltpu.VMEM((seq_count, block_rows, width), jnp.bfloat16),
             pltpu.VMEM((mp_count, seq_count, block_rows, width), jnp.bfloat16),
             pltpu.VMEM((length, features), jnp.bfloat16),
@@ -503,9 +533,9 @@
             dma((seq_count,)),
             dma((GROUPS, mp_count - 1)),
             dma((GROUPS, mp_count)),
-            dma((pairs, mp_count - 1)),
-            dma((pairs, mp_count)),
-            dma((4,)),
+            dma((pairs, 2, mp_count - 1)),
+            dma((pairs, 2, mp_count)),
+            dma((6,)),
         ],
         compiler_params=pltpu.CompilerParams(
             collective_id=0, has_side_effects=True, vmem_limit_bytes=56 * 1024 * 1024
@@ -514,7 +544,7 @@
     )(
         store_rows.reshape(seq_count, block_rows, width),
         norm_gain.reshape(1, features),
-        rel_bias,
+        rel_bias.T,
         lengths,
         slot_map,
         block_passage,

time: 67.9 us -> 62.8 us (0.925); the launches traced: 66.7 us -> 62.6 us
  Pallas kernels: 63 us -> 60.3 us
  local copies, waits for them, and re-layouts: 3.63 us -> 2.26 us
    pallas_call x1, Pallas kernels: 63 us -> 60.3 us  [on_device(): pl.pallas_call(body, out_shape=jax.ShapeDtypeStruct((length, width), jnp....]
    unnamed x2 -> x1, local copies, waits for them, and re-layouts: 3.63 us -> 2.26 us
where the time goes in v1:
time: 62.8 us; the launch traced here: 62.6 us
  Pallas kernels  60.3 us (96%)
  local copies, waits for them, and re-layouts  2.26 us (4%)
    pallas_call x1, Pallas kernels, on_device(): pl.pallas_call(body, out_shape=jax.ShapeDtypeStruct((length, width), jnp....  60.3 us
    unnamed x1, local copies, waits for them, and re-layouts  2.26 us

profile of v1, /device:TPU:11, one launch (start us, length us, event | category | flops | bytes accessed | tf_op | source)
XLA Modules:
  0.0 62.6 jit_solution(7514156435738267470)
XLA Ops:
  0.0 60.3 %encoder.1 = bf16[512,1024]{1,0:T(8,128)(2,1)} custom-call(bf16[8,64,1024]{2,1,0:T(8,128)(2,1)} %bitcast.3, f32[1,4096]{1,0:T(1,128)} %bitcast.4, f32[8,32]{1,0:T(8,128)} %bitcast.5, s32[8]{0:T(128)} %refs_3_.1, s32[8]{0:T(128)} %refs_4_.1, s32[8,8]{1,0:T(8,128)} %refs_5_.1, s32[8,8]{1,0:T(8,128)} %refs_6_.1, bf16[4096,512]{1,0:T(8,128)(2,1)} %refs_7_.1, ...), custom_call_target="tpu_custom_call" | custom-call | tf_op jit(solution)/shard_map/encoder/pallas_call | solution.py:511
  60.3 2.3 %copy.13 = bf16[512,1024]{1,0:T(8,128)(2,1)} copy(bf16[512,1024]{1,0:T(8,128)(2,1)} %encoder.1) | data formatting | bytes 2097152

commit v2 on v1

--- a/solution.py
+++ b/solution.py
@@ -196,10 +196,10 @@
     far = list(range(half_slots, seq_count))
     order = []
     while near or far:
+        if far:
+            order.append(far.pop(0))
         if near:
             order.append(near.pop(0))
-        if far:
-            order.append(far.pop(0))
     if per_group == 1:
         handle(0)
     for step in order:

time: 62.8 us -> 65.6 us (1.045)
  Pallas kernels: 60.3 us -> 63.1 us
    pallas_call x1, Pallas kernels: 60.3 us -> 63.1 us  [on_device(): pl.pallas_call(body, out_shape=jax.ShapeDtypeStruct((length, width), jnp....]
where the time goes in v2:
time: 65.6 us; the launch traced here: 65.4 us
  Pallas kernels  63.1 us (96%)
  local copies, waits for them, and re-layouts  2.26 us (3%)
    pallas_call x1, Pallas kernels, on_device(): pl.pallas_call(body, out_shape=jax.ShapeDtypeStruct((length, width), jnp....  63.1 us
    unnamed x1, local copies, waits for them, and re-layouts  2.26 us

profile of v2, /device:TPU:11, one launch (start us, length us, event | category | flops | bytes accessed | tf_op | source)
XLA Modules:
  0.0 65.4 jit_solution(3914241853590132771)
XLA Ops:
  0.0 63.1 %encoder.1 = bf16[512,1024]{1,0:T(8,128)(2,1)} custom-call(bf16[8,64,1024]{2,1,0:T(8,128)(2,1)} %bitcast.3, f32[1,4096]{1,0:T(1,128)} %bitcast.4, f32[8,32]{1,0:T(8,128)} %bitcast.5, s32[8]{0:T(128)} %refs_3_.1, s32[8]{0:T(128)} %refs_4_.1, s32[8,8]{1,0:T(8,128)} %refs_5_.1, s32[8,8]{1,0:T(8,128)} %refs_6_.1, bf16[4096,512]{1,0:T(8,128)(2,1)} %refs_7_.1, ...), custom_call_target="tpu_custom_call" | custom-call | tf_op jit(solution)/shard_map/encoder/pallas_call | solution.py:511
  63.1 2.3 %copy.13 = bf16[512,1024]{1,0:T(8,128)(2,1)} copy(bf16[512,1024]{1,0:T(8,128)(2,1)} %encoder.1) | data formatting | bytes 2097152
